TPU v7x, 512 devices: a whole 4x4x16 slice. The times are simulated.
512 devices in a mesh: ctx: 128 (over y, x, z_lo), tp: 4 (over z_hi, core).
Axes of the slice: x: 4, y: 4, z: 16 (z_hi: 2, z_lo: 8; z = z_hi * 8 + z_lo), core: 2. Of those that a mesh axis runs over, the one named last changes fastest.
Arguments:
- hidden: bfloat16 [32768, 8192], P('ctx', 'tp'), may hold values from -6 to 6
- queries: bfloat16 [32768, 4096], P('ctx', 'tp'), may hold values from -1000 to 1000
- kv_weight: bfloat16 [8192, 1024], P('tp', 'ctx'), may hold values from -0.0625 to 0.0625
- kv_bias: bfloat16 [1024], P('tp'), may hold values from -3 to 3
- window: int32 [4], P('tp'), may hold values from 1024 to 4096, as said below
- segment_ids: int32 [32768], P('ctx'), may hold values from 0 to 15, never falling along the last dimension, each value on 1 to 4096 neighbouring positions
Outputs:
- attended: bfloat16 [32768, 4096], P('ctx', 'tp')
- kv_cache: bfloat16 [32768, 1024], P('ctx', 'tp')
Inputs may be any that keep to these rules, and one draw needn't show every extreme that they name: `window`: each entry is 1024 to 4096; some key head's entry equals 4096.
All inputs are finite; a program needn't handle non-finite values.
Results may differ from a plain program's by a relative error of at most 0.012.
Values may be sent and summed in bfloat16 or wider, within the bound.
No kernel may reach another device: no remote copies, remote signals or barrier semaphores. Data moves between devices by JAX's collectives and lax.ppermute only.
A program may use at most 64 MiB of HBM per device.

v0:
```python
import jax
import jax.numpy as jnp
from jax import lax
from jax.sharding import PartitionSpec as P

WINDOW = 4096


rope_base = 1000000.0


def split_up(array, dim, count):
    dims = array.shape
    tiles = array.reshape(*dims[:dim], count, dims[dim] // count, *dims[dim + 1 :])
    return jnp.moveaxis(tiles, dim, 0)


def sent_and_summed(array, axis, dim):
    count = lax.axis_size(axis)
    tiles = lax.all_to_all(split_up(array, dim, count), axis, 0, 0, tiled=True)
    return jnp.sum(tiles, axis=0)


def passed_along(value, axis, steps):
    count = lax.axis_size(axis)
    initial, last = (max(0, -steps), min(count, count - steps))
    return lax.ppermute(value, axis, [(source, source + steps) for source in range(initial, last)])


def rotate(values, positions):
    half = values.shape[-1] // 2
    freqs = rope_base ** (-2.0 * jnp.arange(half, dtype=jnp.float32) / values.shape[-1])
    angles = positions.astype(jnp.float32)[:, None] * freqs[None, :]
    cosine = jnp.cos(angles)
    sine = jnp.sin(angles)
    former = values[:, :half]
    latter = values[:, half:]
    return jnp.concatenate(
        [former * cosine - latter * sine, latter * cosine + former * sine], axis=1
    )


def attend(carry, query_rows, query_pos, query_seg, reach, block, block_seg, block_pos):
    running_max, running_sum, weighted = carry
    head = block.shape[1] // 2
    scores = lax.dot_general(
        query_rows, block[:, :head], (((1,), (1,)), ((), ())), preferred_element_type=jnp.float32
    )
    scores = scores * head ** (-0.5)
    gap = query_pos[:, None] - block_pos[None, :]
    allowed = (
        (query_seg[:, None] == block_seg[None, :])
        & (gap >= 0)
        & (gap < reach)
        & (block_pos >= 0)[None, :]
    )
    scores = jnp.where(allowed, scores, -jnp.inf)
    newest = jnp.maximum(running_max, jnp.max(scores, axis=1))
    probs = jnp.exp(scores - newest[:, None])
    rescale = jnp.exp(running_max - newest)
    summed = running_sum * rescale + jnp.sum(probs, axis=1)
    mixed = jnp.dot(probs.astype(jnp.bfloat16), block[:, head:], preferred_element_type=jnp.float32)
    return (newest, summed, weighted * rescale[:, None] + mixed)


def body(hidden, queries, kv_weight, kv_bias, window, segment_ids):
    tok_rows = hidden.shape[0]
    terms = jnp.dot(
        hidden,
        lax.all_gather(kv_weight, "ctx", axis=1, tiled=True),
        preferred_element_type=jnp.float32,
    )
    projected = sent_and_summed(terms, "tp", 1)
    projected = projected + kv_bias.astype(jnp.float32)[None, :]
    head = kv_bias.shape[0] // 2
    shard = lax.axis_index("ctx")
    offsets = jnp.arange(tok_rows, dtype=jnp.int32)
    positions = shard * tok_rows + offsets
    cache = jnp.concatenate(
        [rotate(projected[:, :head], positions), projected[:, head:]], axis=1
    ).astype(jnp.bfloat16)
    group = queries.shape[1] // head
    query_rows = queries.reshape(tok_rows * group, head)
    query_pos = jnp.repeat(positions, group)
    query_seg = jnp.repeat(segment_ids, group)
    reach = window[0]

    def absorb(carry, block, block_seg, block_pos):
        return attend(carry, query_rows, query_pos, query_seg, reach, block, block_seg, block_pos)

    row_count = tok_rows * group
    carry = (
        jnp.full((row_count,), -jnp.inf, jnp.float32),
        jnp.zeros((row_count,), jnp.float32),
        jnp.zeros((row_count, head), jnp.float32),
    )
    carry = absorb(carry, cache, segment_ids, positions)
    halo_count = WINDOW // tok_rows
    held_kv = cache
    held_seg = segment_ids
    have = 0
    while have < halo_count:
        got_kv, got_seg = passed_along((held_kv, held_seg), "ctx", max(have, 1))
        shards = got_kv.shape[0] // tok_rows
        for member in range(shards):
            lower = member * tok_rows
            block_pos = (shard - have - shards + member) * tok_rows + offsets
            carry = absorb(
                carry,
                got_kv[lower : lower + tok_rows],
                got_seg[lower : lower + tok_rows],
                block_pos,
            )
        if have == 0:
            held_kv, held_seg = (got_kv, got_seg)
        else:
            held_kv = jnp.concatenate([got_kv, held_kv], axis=0)
            held_seg = jnp.concatenate([got_seg, held_seg], axis=0)
        have = have + shards
    newest, summed, weighted = carry
    attended = (weighted / summed[:, None]).reshape(tok_rows, group * head).astype(jnp.bfloat16)
    return (attended, cache)


def solution(mesh):
    in_specs = (P("ctx", "tp"), P("ctx", "tp"), P("tp", "ctx"), P("tp"), P("tp"), P("ctx"))
    out_specs = (P("ctx", "tp"), P("ctx", "tp"))
    return jax.shard_map(body, mesh=mesh, in_specs=in_specs, out_specs=out_specs, check_vma=False)
```

profile of v0, /device:TPU:6, one launch (start us, length us, event | category | flops | bytes accessed | tf_op | source)
XLA Modules:
  0.0 1186.3 jit_solution(4037237898657685963)
XLA Ops:
  7.9 3.8 collective-permute-start
  12.0 875.0 %all-gather.2.cloned.1.call-done = bf16[2048,1024]{0,1:T(8,128)(2,1)} async-done(((bf16[2048,8]{0,1:T(8,128)(2,1)}), bf16[2048,1024]{0,1:T(8,128)(2,1)}) %all-gather.2.cloned.1.call-update) | async-done | bytes 4194320 | tf_op jit(solution)/shard_map/all_gather | solution.py:70
  886.9 3.5 fusion.267
  890.5 1.1 copy.11
  891.5 11.3 all-to-all-start
  903.0 4.4 collective-permute-start.2
  907.4 13.4 %collective-permute-done.2 = s32[256]{0:T(256)S(1)} collective-permute-done((s32[256]{0:T(256)S(1)}, s32[256]{0:T(256)S(1)}, u32[]{:S(2)}, u32[]{:S(2)}) %collective-permute-start.2) | collective-permute-done | bytes 1056 | tf_op jit(solution)/shard_map/ppermute | solution.py:27
  920.8 10.0 collective-permute-start.4
  933.2 28.8 %collective-permute-start.6 = (s32[1024]{0:T(1024)S(1)}, s32[1024]{0:T(1024)S(1)}, u32[]{:S(2)}, u32[]{:S(2)}) collective-permute-start(s32[1024]{0:T(1024)S(1)} %pad_add_fusion.1), channel_id=1, source_target_pairs={{0,16},{4,20},{8,24},{12,28},{16,32},{20,36},{24,40},{28,44},{32,4... | collective-permute-start | bytes 12296 | tf_op jit(solution)/shard_map/ppermute | solution.py:27
  962.0 10.0 collective-permute-done.6
  972.0 18.4 %collective-permute-start.8 = (s32[2048]{0:T(1024)S(1)}, s32[2048]{0:T(1024)S(1)}, u32[]{:S(2)}, u32[]{:S(2)}) collective-permute-start(s32[2048]{0:T(1024)S(1)} %pad_add_fusion), channel_id=1, source_target_pairs={{0,32},{4,36},{8,40},{12,44},{16,48},{20,52},{24,56},{28,60},{32,6... | collective-permute-start | bytes 24584 | tf_op jit(solution)/shard_map/ppermute | solution.py:27
  990.3 15.1 %collective-permute-done.8 = s32[2048]{0:T(1024)S(1)} collective-permute-done((s32[2048]{0:T(1024)S(1)}, s32[2048]{0:T(1024)S(1)}, u32[]{:S(2)}, u32[]{:S(2)}) %collective-permute-start.8) | collective-permute-done | bytes 8224 | tf_op jit(solution)/shard_map/ppermute | solution.py:27
  1006.3 4.3 collective-permute-start.1
  1010.6 1.0 fusion.264
  1012.0 8.7 collective-permute-done.1
  1020.7 1.9 collective-permute-start.3
  1023.6 12.8 %collective-permute-done.3 = bf16[256,256]{1,0:T(8,128)(2,1)S(1)} collective-permute-done((bf16[256,256]{1,0:T(8,128)(2,1)S(1)}, bf16[256,256]{1,0:T(8,128)(2,1)S(1)}, u32[]{:S(2)}, u32[]{:S(2)}) %collective-permute-start.3) | collective-permute-done | bytes 131104 | tf_op jit(solution)/shard_map/ppermute | solution.py:27
  1036.4 1.9 collective-permute-start.5
  1039.3 17.8 %collective-permute-done.5 = bf16[512,256]{1,0:T(8,128)(2,1)S(1)} collective-permute-done((bf16[512,256]{1,0:T(8,128)(2,1)S(1)}, bf16[512,256]{1,0:T(8,128)(2,1)S(1)}, u32[]{:S(2)}, u32[]{:S(2)}) %collective-permute-start.5) | collective-permute-done | bytes 262176 | tf_op jit(solution)/shard_map/ppermute | solution.py:27
  1057.1 1.9 collective-permute-start.7
  1061.1 35.2 %collective-permute-done.7 = bf16[1024,256]{1,0:T(8,128)(2,1)S(1)} collective-permute-done((bf16[1024,256]{1,0:T(8,128)(2,1)S(1)}, bf16[1024,256]{1,0:T(8,128)(2,1)S(1)}, u32[]{:S(2)}, u32[]{:S(2)}) %collective-permute-start.7) | collective-permute-done | bytes 524320 | tf_op jit(solution)/shard_map/ppermute | solution.py:27
  1096.3 2.1 collective-permute-start.9
  1102.4 48.9 %collective-permute-done.9 = bf16[2048,256]{1,0:T(8,128)(2,1)S(1)} collective-permute-done((bf16[2048,256]{1,0:T(8,128)(2,1)S(1)}, bf16[2048,256]{1,0:T(8,128)(2,1)S(1)}, u32[]{:S(2)}, u32[]{:S(2)}) %collective-permute-start.9) | collective-permute-done | bytes 1048608 | tf_op jit(solution)/shard_map/ppermute | solution.py:27
  1173.4 5.1 fusion.63
  (117 shorter events, 34.7 us)
Async XLA Ops:
  7.2 879.8 %copy-start = (bf16[256,2048]{1,0:T(8,128)(2,1)S(1)}, bf16[256,2048]{1,0:T(8,128)(2,1)}, u32[]{:S(2)}) copy-start(bf16[256,2048]{1,0:T(8,128)(2,1)} %param.6) | copy-start | bytes 3145732
  7.2 879.8 %all-gather.2.cloned.1.call-start = ((), (), s32[]{:S(2)}) async-start(), calls=%async_computation.1 | async-start | bytes 4227072 | tf_op jit(solution)/shard_map/all_gather | solution.py:70
  7.9 895.1 %collective-permute-start = (s32[256]{0:T(256)}, s32[256]{0:T(256)S(1)}, u32[]{:S(2)}, u32[]{:S(2)}) collective-permute-start(s32[256]{0:T(256)} %param.11), channel_id=1, source_target_pairs={{0,4},{4,8},{8,12},{12,16},{16,20},{20,24},{24,28},{28,32},{32,36}... | collective-permute-start | bytes 3080 | tf_op jit(solution)/shard_map/ppermute | solution.py:27
  890.4 41.1 %copy-start.5 = (bf16[256]{0:T(256)(128)(2,1)S(1)}, bf16[256]{0:T(256)(128)(2,1)}, u32[]{:S(2)}) copy-start(bf16[256]{0:T(256)(128)(2,1)} %param.9) | copy-start | bytes 1540
  890.4 41.3 %copy-start.4 = (s32[256]{0:T(256)S(1)}, s32[256]{0:T(256)}, u32[]{:S(2)}) copy-start(s32[256]{0:T(256)} %param.11) | copy-start | bytes 3076
  890.4 41.5 %copy-start.2 = (bf16[256,1024]{1,0:T(8,128)(2,1)S(1)}, bf16[256,1024]{1,0:T(8,128)(2,1)}, u32[]{:S(2)}) copy-start(bf16[256,1024]{1,0:T(8,128)(2,1)} %param.7) | copy-start | bytes 1572868
  891.5 113.9 %all-to-all-start = ((f32[4,256,256]{2,1,0:T(8,128)}), f32[4,256,256]{2,1,0:T(8,128)S(1)}, u32[]{:S(2)}, u32[]{:S(2)}) async-start(f32[4,256,256]{2,1,0:T(8,128)} %bitcast.94), calls=%async_computation | async-start | bytes 2097152 | tf_op jit(solution)/shard_map/all_to_all | solution.py:20
  903.0 17.8 %collective-permute-start.2 = (s32[256]{0:T(256)S(1)}, s32[256]{0:T(256)S(1)}, u32[]{:S(2)}, u32[]{:S(2)}) collective-permute-start(s32[256]{0:T(256)S(1)} %collective-permute-done), channel_id=1, source_target_pairs={{0,4},{4,8},{8,12},{12,16},{16,20},{20,24},{24,28},{28,32},{32,36}... | collective-permute-start | bytes 3080 | tf_op jit(solution)/shard_map/ppermute | solution.py:27
  920.8 12.3 %collective-permute-start.4 = (s32[512]{0:T(512)S(1)}, s32[512]{0:T(512)S(1)}, u32[]{:S(2)}, u32[]{:S(2)}) collective-permute-start(s32[512]{0:T(512)S(1)} %pad_add_fusion.2), channel_id=1, source_target_pairs={{0,8},{4,12},{8,16},{12,20},{16,24},{20,28},{24,32},{28,36},{32,40... | collective-permute-start | bytes 6152 | tf_op jit(solution)/shard_map/ppermute | solution.py:27
  933.2 38.8 %collective-permute-start.6 = (s32[1024]{0:T(1024)S(1)}, s32[1024]{0:T(1024)S(1)}, u32[]{:S(2)}, u32[]{:S(2)}) collective-permute-start(s32[1024]{0:T(1024)S(1)} %pad_add_fusion.1), channel_id=1, source_target_pairs={{0,16},{4,20},{8,24},{12,28},{16,32},{20,36},{24,40},{28,44},{32,4... | collective-permute-start | bytes 12296 | tf_op jit(solution)/shard_map/ppermute | solution.py:27
  972.0 33.5 %collective-permute-start.8 = (s32[2048]{0:T(1024)S(1)}, s32[2048]{0:T(1024)S(1)}, u32[]{:S(2)}, u32[]{:S(2)}) collective-permute-start(s32[2048]{0:T(1024)S(1)} %pad_add_fusion), channel_id=1, source_target_pairs={{0,32},{4,36},{8,40},{12,44},{16,48},{20,52},{24,56},{28,60},{32,6... | collective-permute-start | bytes 24584 | tf_op jit(solution)/shard_map/ppermute | solution.py:27
  1006.3 5.4 copy-start.3
  1006.3 14.4 %collective-permute-start.1 = (bf16[256,256]{1,0:T(8,128)(2,1)S(1)}, bf16[256,256]{1,0:T(8,128)(2,1)S(1)}, u32[]{:S(2)}, u32[]{:S(2)}) collective-permute-start(bf16[256,256]{1,0:T(8,128)(2,1)S(1)} %pad_maximum_fusion.3), channel_id=1, source_target_pairs={{0,4},{4,8},{8,12},{12,16},{16,20},{20,24},{24,28},{28,32},{32,36}... | collective-permute-start | bytes 393224 | tf_op jit(solution)/shard_map/ppermute | solution.py:27
  1020.7 15.8 %collective-permute-start.3 = (bf16[256,256]{1,0:T(8,128)(2,1)S(1)}, bf16[256,256]{1,0:T(8,128)(2,1)S(1)}, u32[]{:S(2)}, u32[]{:S(2)}) collective-permute-start(bf16[256,256]{1,0:T(8,128)(2,1)S(1)} %collective-permute-done.1), channel_id=1, source_target_pairs={{0,4},{4,8},{8,12},{12,16},{16,20},{20,24},{24,28},{28,32},{32,36}... | collective-permute-start | bytes 393224 | tf_op jit(solution)/shard_map/ppermute | solution.py:27
  1036.4 20.7 %collective-permute-start.5 = (bf16[512,256]{1,0:T(8,128)(2,1)S(1)}, bf16[512,256]{1,0:T(8,128)(2,1)S(1)}, u32[]{:S(2)}, u32[]{:S(2)}) collective-permute-start(bf16[512,256]{1,0:T(8,128)(2,1)S(1)} %pad_maximum_fusion.2), channel_id=1, source_target_pairs={{0,8},{4,12},{8,16},{12,20},{16,24},{20,28},{24,32},{28,36},{32,40... | collective-permute-start | bytes 786440 | tf_op jit(solution)/shard_map/ppermute | solution.py:27
  1057.1 39.1 %collective-permute-start.7 = (bf16[1024,256]{1,0:T(8,128)(2,1)S(1)}, bf16[1024,256]{1,0:T(8,128)(2,1)S(1)}, u32[]{:S(2)}, u32[]{:S(2)}) collective-permute-start(bf16[1024,256]{1,0:T(8,128)(2,1)S(1)} %pad_maximum_fusion.1), channel_id=1, source_target_pairs={{0,16},{4,20},{8,24},{12,28},{16,32},{20,36},{24,40},{28,44},{32,4... | collective-permute-start | bytes 1572872 | tf_op jit(solution)/shard_map/ppermute | solution.py:27
  1096.3 55.0 %collective-permute-start.9 = (bf16[2048,256]{1,0:T(8,128)(2,1)S(1)}, bf16[2048,256]{1,0:T(8,128)(2,1)S(1)}, u32[]{:S(2)}, u32[]{:S(2)}) collective-permute-start(bf16[2048,256]{1,0:T(8,128)(2,1)S(1)} %pad_maximum_fusion), channel_id=1, source_target_pairs={{0,32},{4,36},{8,40},{12,44},{16,48},{20,52},{24,56},{28,60},{32,6... | collective-permute-start | bytes 3145736 | tf_op jit(solution)/shard_map/ppermute | solution.py:27
  1173.4 6.1 copy-start.1
Sparse Core Ops, SparseCore 0:
  10.1 876.8 all-gather.1
where the time goes:
time: 1190 us
  waiting for transfers between devices  1040 us (87%)
  starting transfers between devices  88.8 us (7%)
  matrix products  34.4 us (3%)
  between operations  15.4 us (1%)
    all_gather x1, waiting for transfers between devices, body(): lax.all_gather(kv_weight, 'ctx', axis=1, tiled=True)  875 us
    ppermute x10, waiting for transfers between devices, passed_along(): lax.ppermute(value, axis, [(source, source + steps) for source in range(i...  163 us
    ppermute x10, starting transfers between devices, passed_along(): lax.ppermute(value, axis, [(source, source + steps) for source in range(i...  77.4 us
  transfers between devices with their start and end apart: 12, of which 10 were waited for; matrix products, arithmetic and copies ran while one was open for 1% of the time, Pallas kernels for 0%

commit v1 on v0

v1 whole, which is shorter than its diff:
```python
import jax
import jax.numpy as jnp
from jax import lax
from jax.sharding import Mesh, PartitionSpec as P

rope_base = 1000000.0
NY, NX, NZ = 4, 4, 8
ROWS = NY * NX
SEGS = 16


def gathered(part, axis, count):
    copies = jnp.broadcast_to(part[None], (count,) + part.shape)
    return lax.all_to_all(copies, axis, 0, 0, tiled=True)


def next_row(value):
    return lax.ppermute(value, ("y", "x"), [(i, i + 1) for i in range(ROWS - 1)])


def rotate(values, positions):
    half = values.shape[-1] // 2
    freqs = rope_base ** (-2.0 * jnp.arange(half, dtype=jnp.float32) / values.shape[-1])
    angles = positions.astype(jnp.float32)[:, None] * freqs[None, :]
    cosine = jnp.cos(angles)
    sine = jnp.sin(angles)
    former = values[:, :half]
    latter = values[:, half:]
    return jnp.concatenate(
        [former * cosine - latter * sine, latter * cosine + former * sine], axis=1
    )


def attend(carry, query_rows, query_pos, query_start, block, block_pos):
    running_max, running_sum, weighted = carry
    head = block.shape[1] // 2
    scores = lax.dot_general(
        query_rows, block[:, :head], (((1,), (1,)), ((), ())), preferred_element_type=jnp.float32
    )
    scores = scores * head ** (-0.5)
    allowed = (block_pos[None, :] >= query_start[:, None]) & (
        block_pos[None, :] <= query_pos[:, None]
    )
    scores = jnp.where(allowed, scores, -jnp.inf)
    newest = jnp.maximum(running_max, jnp.max(scores, axis=1))
    probs = jnp.exp(scores - newest[:, None])
    rescale = jnp.exp(running_max - newest)
    summed = running_sum * rescale + jnp.sum(probs, axis=1)
    mixed = jnp.dot(probs.astype(jnp.bfloat16), block[:, head:], preferred_element_type=jnp.float32)
    return (newest, summed, weighted * rescale[:, None] + mixed)


def body(hidden, queries, kv_weight, kv_bias, window, segment_ids):
    tok_rows = hidden.shape[0]
    feats = hidden.shape[1]
    head = kv_bias.shape[0] // 2
    z = lax.axis_index("zl")
    row = lax.axis_index("y") * NX + lax.axis_index("x")
    zh = lax.axis_index("zh")
    core = lax.axis_index("core")
    shard = row * NZ + z
    positions = shard * tok_rows + jnp.arange(tok_rows, dtype=jnp.int32)

    below = jnp.sum(
        (segment_ids[:, None] < jnp.arange(SEGS, dtype=jnp.int32)[None, :]).astype(jnp.int32), axis=0
    )
    doc_start = lax.psum(below, ("y", "x", "zl"))
    token_start = jnp.sum(
        jnp.where(
            segment_ids[:, None] == jnp.arange(SEGS, dtype=jnp.int32)[None, :], doc_start[None, :], 0
        ),
        axis=1,
    )
    token_start = jnp.maximum(token_start, positions - window[0] + 1)

    line = gathered(kv_weight.T, "zl", NZ)
    half = feats // 2
    first = line[:, :, :half]
    second = line[:, :, half:]
    first = gathered(first, "x", NX)
    second = gathered(second, "y", NY)
    first = gathered(first, "y", NY).reshape(-1, half)
    second = gathered(second, "x", NX)
    second = jnp.swapaxes(second, 0, 1).reshape(-1, half)
    last_dims = (((1,), (1,)), ((), ()))
    terms = lax.dot_general(
        hidden[:, :half], first, last_dims, preferred_element_type=jnp.float32
    ) + lax.dot_general(hidden[:, half:], second, last_dims, preferred_element_type=jnp.float32)

    width = 2 * head
    quarter = [terms[:, g * width : (g + 1) * width] for g in range(4)]
    lower = core == 0
    sent = jnp.concatenate(
        [jnp.where(lower, quarter[1], quarter[0]), jnp.where(lower, quarter[3], quarter[2])], axis=1
    )
    kept = jnp.concatenate(
        [jnp.where(lower, quarter[0], quarter[1]), jnp.where(lower, quarter[2], quarter[3])], axis=1
    )
    chip = kept + lax.ppermute(sent, "core", [(0, 1), (1, 0)])
    near = zh == 0
    far = jnp.where(near, chip[:, width:], chip[:, :width]).astype(jnp.bfloat16)
    far = lax.ppermute(far, "zh", [(0, 1), (1, 0)])
    projected = jnp.where(near, chip[:, :width], chip[:, width:]) + far.astype(jnp.float32)
    projected = projected + kv_bias.astype(jnp.float32)[None, :]
    cache = jnp.concatenate(
        [rotate(projected[:, :head], positions), projected[:, head:]], axis=1
    ).astype(jnp.bfloat16)

    older = next_row(cache)
    slots = jnp.arange(NZ, dtype=jnp.int32)
    outgoing = jnp.where((slots >= z)[:, None, None], cache[None], older[None])
    recent = lax.all_to_all(outgoing, "zl", 0, 0, tiled=True)
    earlier = next_row(jnp.concatenate([recent, older[None]], axis=0))
    recent_shard = jnp.where(slots <= z, row * NZ, (row - 1) * NZ) + slots
    offsets = jnp.arange(tok_rows, dtype=jnp.int32)

    group = queries.shape[1] // head
    query_rows = queries.reshape(tok_rows * group, head)
    query_pos = jnp.repeat(positions, group)
    query_start = jnp.repeat(token_start, group)
    row_count = tok_rows * group
    carry = (
        jnp.full((row_count,), -1e30, jnp.float32),
        jnp.zeros((row_count,), jnp.float32),
        jnp.zeros((row_count, head), jnp.float32),
    )
    for slot in range(NZ):
        block_pos = recent_shard[slot] * tok_rows + offsets
        carry = attend(carry, query_rows, query_pos, query_start, recent[slot], block_pos)
    for slot in range(NZ):
        block_pos = (recent_shard[slot] - NZ) * tok_rows + offsets
        carry = attend(carry, query_rows, query_pos, query_start, earlier[slot], block_pos)
    block_pos = (shard - 2 * NZ) * tok_rows + offsets
    carry = attend(carry, query_rows, query_pos, query_start, earlier[NZ], block_pos)
    newest, summed, weighted = carry
    attended = (weighted / summed[:, None]).reshape(tok_rows, group * head).astype(jnp.bfloat16)
    return (attended, cache)


def solution(mesh):
    fine = Mesh(mesh.devices.reshape(NY, NX, NZ, 2, 2), ("y", "x", "zl", "zh", "core"))
    ctx, tp = ("y", "x", "zl"), ("zh", "core")
    in_specs = (P(ctx, tp), P(ctx, tp), P(tp, ctx), P(tp), P(tp), P(ctx))
    out_specs = (P(ctx, tp), P(ctx, tp))
    return jax.shard_map(body, mesh=fine, in_specs=in_specs, out_specs=out_specs, check_vma=False)
```

time: 1190 us -> 268 us (0.23)
  waiting for transfers between devices: 1040 us -> 43.9 us
  blocking collectives: 0 us -> 128 us
  starting transfers between devices: 88.8 us -> 43.3 us
    all_gather x1 -> x0, waiting for transfers between devices: 875 us -> none  [body(): lax.all_gather(kv_weight, 'ctx', axis=1, tiled=True)]
    ppermute x10 -> x4, waiting for transfers between devices: 163 us -> 29.9 us  [the longest x2 20.1 us: next_row(): lax.ppermute(value, ('y', 'x'), [(i, i + 1) for i in range(ROWS - 1)])]
    all_to_all x0 -> x4, blocking collectives: none -> 73.4 us  [gathered(): return lax.all_to_all(copies, axis, 0, 0, tiled=True)]
    ppermute x10 -> x4, starting transfers between devices: 77.4 us -> 16.2 us  [the longest x1 8.22 us: body(): far = lax.ppermute(far, 'zh', [(0, 1), (1, 0)])]
    psum x0 -> x1, blocking collectives: none -> 54.1 us  [body(): doc_start = lax.psum(below, ('y', 'x', 'zl'))]
    all_to_all x1 -> x2, starting transfers between devices: 11.3 us -> 27.1 us  [the longest x1 20.6 us: body(): recent = lax.all_to_all(outgoing, 'zl', 0, 0, tiled=True)]
    all_to_all x1 -> x2, waiting for transfers between devices: 0.01 us -> 14 us  [the longest x1 14 us: gathered(): return lax.all_to_all(copies, axis, 0, 0, tiled=True)]
  transfers between devices with their start and end apart: 12 -> 6, of which waited for: 10 -> 5; matrix products, arithmetic and copies ran while one was open for 1% -> 3% of each run, Pallas kernels for 0% -> 0%
where the time goes in v1:
time: 268 us; the launch traced here: 266 us
  blocking collectives  128 us (48%)
  waiting for transfers between devices  43.9 us (16%)
  starting transfers between devices  43.3 us (16%)
  matrix products  24.6 us (9%)
  between operations  12 us (4%)
  other arithmetic  7.82 us (3%)
  local copies, waits for them, and re-layouts  7.29 us (3%)
    all_to_all x4, blocking collectives, gathered(): return lax.all_to_all(copies, axis, 0, 0, tiled=True)  73.4 us
    psum x1, blocking collectives, body(): doc_start = lax.psum(below, ('y', 'x', 'zl'))  54.1 us
    all_to_all x1, starting transfers between devices, body(): recent = lax.all_to_all(outgoing, 'zl', 0, 0, tiled=True)  20.6 us
    ppermute x2, waiting for transfers between devices, next_row(): lax.ppermute(value, ('y', 'x'), [(i, i + 1) for i in range(ROWS - 1)])  20.1 us
    all_to_all x1, waiting for transfers between devices, gathered(): return lax.all_to_all(copies, axis, 0, 0, tiled=True)  14 us
    dot_general x17, matrix products, attend(): jnp.dot(probs.astype(jnp.bfloat16), block[:, head:], preferred_element_ty...  11.7 us
    dot_general x17, matrix products, attend(): lax.dot_general(query_rows, block[:, :head], (((1,), (1,)), ((), ())), pr...  10.3 us
    ppermute x1, starting transfers between devices, body(): far = lax.ppermute(far, 'zh', [(0, 1), (1, 0)])  8.22 us
  transfers between devices with their start and end apart: 6, of which 5 were waited for; matrix products, arithmetic and copies ran while one was open for 3% of the time, Pallas kernels for 0%

profile of v1, /device:TPU:6, one launch (start us, length us, event | category | flops | bytes accessed | tf_op | source)
XLA Modules:
  0.0 266.4 jit_solution(2545550122505455489)
XLA Ops:
  0.6 0.8 broadcast_in_dim.92
  1.4 29.0 %all_to_all.30 = bf16[8,8,2048]{2,1,0:T(8,128)(2,1)S(1)} all-to-all(bf16[8,8,2048]{2,1,0:T(8,128)(2,1)S(1)} %broadcast_in_dim.92), channel_id=1, replica_groups=mesh['y'=4,'x'=4,'zl'=8,'zh'=2,'core'=2] {'zl'}, dimensions={0} | all-to-all | bytes 524288 | tf_op jit(solution)/shard_map/all_to_all | solution.py:14
  30.5 12.3 %all_to_all.31 = bf16[4,8,8,1024]{3,2,1,0:T(8,128)(2,1)S(1)} all-to-all(bf16[4,8,8,1024]{3,2,1,0:T(8,128)(2,1)S(1)} %broadcast_in_dim.95), channel_id=1, replica_groups=mesh['y'=4,'x'=4,'zl'=8,'zh'=2,'core'=2] {'y'}, dimensions={0} | all-to-all | bytes 1048576 | tf_op jit(solution)/shard_map/all_to_all | solution.py:14
  42.9 10.6 %all_to_all.32 = bf16[4,8,8,1024]{3,2,1,0:T(8,128)(2,1)S(1)} all-to-all(bf16[4,8,8,1024]{3,2,1,0:T(8,128)(2,1)S(1)} %broadcast_in_dim.93), channel_id=1, replica_groups=mesh['y'=4,'x'=4,'zl'=8,'zh'=2,'core'=2] {'x'}, dimensions={0} | all-to-all | bytes 1048576 | tf_op jit(solution)/shard_map/all_to_all | solution.py:14
  53.8 21.5 %all_to_all.33 = bf16[4,4,8,8,1024]{4,3,2,1,0:T(8,128)(2,1)S(1)} all-to-all(bf16[4,4,8,8,1024]{4,3,2,1,0:T(8,128)(2,1)S(1)} %broadcast_in_dim.94), channel_id=1, replica_groups=mesh['y'=4,'x'=4,'zl'=8,'zh'=2,'core'=2] {'y'}, dimensions={0} | all-to-all | bytes 4194304 | tf_op jit(solution)/shard_map/all_to_all | solution.py:14
  75.2 1.6 broadcast_in_dim.96
  76.8 6.5 %all-to-all-start.4 = ((bf16[4,4,8,8,1024]{4,3,2,1,0:T(8,128)(2,1)}), bf16[4,4,8,8,1024]{4,3,2,1,0:T(8,128)(2,1)}, u32[]{:S(2)}, u32[]{:S(2)}) async-start(bf16[4,4,8,8,1024]{4,3,2,1,0:T(8,128)(2,1)} %broadcast_in_dim.96), calls=%async_computation.4 | async-start | bytes 4194304 | tf_op jit(solution)/shard_map/all_to_all | solution.py:14
  83.2 1.8 fusion.121
  85.0 14.0 %all-to-all-done.4 = bf16[4,4,8,8,1024]{4,3,2,1,0:T(8,128)(2,1)} async-done(((bf16[4,4,8,8,1024]{4,3,2,1,0:T(8,128)(2,1)}), bf16[4,4,8,8,1024]{4,3,2,1,0:T(8,128)(2,1)}, u32[]{:S(2)}, u32[]{:S(2)}) %all-to-all-start.4) | async-done | bytes 2097184 | tf_op jit(solution)/shard_map/all_to_all | solution.py:14
  99.1 1.8 copy.10
  101.8 1.9 collective-permute-start
  103.7 1.9 collective-permute-done
  105.7 8.2 %collective-permute-start.1 = (bf16[256,256]{0,1:T(8,128)(2,1)S(1)}, bf16[256,256]{0,1:T(8,128)(2,1)S(1)}, u32[]{:S(2)}, u32[]{:S(2)}) collective-permute-start(bf16[256,256]{0,1:T(8,128)(2,1)S(1)} %select_convert_fusion), channel_id=1, source_target_pairs={{0,2},{2,0},{1,3},{3,1},{4,6},{6,4},{5,7},{7,5},{8,10},{10,8},{9,1... | collective-permute-start | bytes 393224 | tf_op jit(solution)/shard_map/ppermute | solution.py:102
  114.0 7.9 %collective-permute-done.1 = bf16[256,256]{0,1:T(8,128)(2,1)S(1)} collective-permute-done((bf16[256,256]{0,1:T(8,128)(2,1)S(1)}, bf16[256,256]{0,1:T(8,128)(2,1)S(1)}, u32[]{:S(2)}, u32[]{:S(2)}) %collective-permute-start.1) | collective-permute-done | bytes 131104 | tf_op jit(solution)/shard_map/ppermute | solution.py:102
  122.4 4.0 %collective-permute-start.2 = (bf16[256,256]{0,1:T(8,128)(2,1)S(1)}, bf16[256,256]{0,1:T(8,128)(2,1)S(1)}, u32[]{:S(2)}, u32[]{:S(2)}) collective-permute-start(bf16[256,256]{0,1:T(8,128)(2,1)S(1)} %pad_maximum_fusion.2), channel_id=1, source_target_pairs={{0,32},{32,64},{64,96},{96,128},{128,160},{160,192},{192,224},{224... | collective-permute-start | bytes 393224 | tf_op jit(solution)/shard_map/ppermute | solution.py:18
  126.5 2.7 %collective-permute-done.2 = bf16[256,256]{0,1:T(8,128)(2,1)S(1)} collective-permute-done((bf16[256,256]{0,1:T(8,128)(2,1)S(1)}, bf16[256,256]{0,1:T(8,128)(2,1)S(1)}, u32[]{:S(2)}, u32[]{:S(2)}) %collective-permute-start.2) | collective-permute-done | bytes 131104 | tf_op jit(solution)/shard_map/ppermute | solution.py:18
  129.3 1.1 broadcast_select_fusion
  130.5 20.6 %all-to-all-start.5 = ((bf16[8,256,256]{2,1,0:T(8,128)(2,1)}), bf16[8,256,256]{2,1,0:T(8,128)(2,1)S(1)}, u32[]{:S(2)}, u32[]{:S(2)}) async-start(bf16[8,256,256]{2,1,0:T(8,128)(2,1)} %broadcast_select_fusion), calls=%async_computation.5 | async-start | bytes 2097152 | tf_op jit(solution)/shard_map/all_to_all | solution.py:112
  162.5 54.1 %psum.7 = s32[16]{0:T(128)S(1)} all-reduce(s32[16]{0:T(128)S(1)} %convert_reduce_fusion), channel_id=1, replica_groups=mesh['y'=4,'x'=4,'zl'=8,'zh'=2,'core'=2] {'y','x','zl'}, use_global_device_ids=true, to_apply=%region_1.0 | all-reduce | flops 16 | bytes 128 | tf_op jit(solution)/shard_map/psum | solution.py:67
  217.8 2.1 collective-permute-start.3
  224.9 17.4 %collective-permute-done.3 = bf16[9,256,256]{2,1,0:T(8,128)(2,1)S(1)} collective-permute-done((bf16[9,256,256]{2,1,0:T(8,128)(2,1)S(1)}, bf16[9,256,256]{2,1,0:T(8,128)(2,1)S(1)}, u32[]{:S(2)}, u32[]{:S(2)}) %collective-permute-start.3) | collective-permute-done | bytes 1179680 | tf_op jit(solution)/shard_map/ppermute | solution.py:18
  253.5 0.9 fusion.50
  262.4 0.9 fusion.37
  265.3 1.0 convert_element_type.104
  (112 shorter events, 29.8 us)
Async XLA Ops:
  76.8 22.3 %all-to-all-start.4 = ((bf16[4,4,8,8,1024]{4,3,2,1,0:T(8,128)(2,1)}), bf16[4,4,8,8,1024]{4,3,2,1,0:T(8,128)(2,1)}, u32[]{:S(2)}, u32[]{:S(2)}) async-start(bf16[4,4,8,8,1024]{4,3,2,1,0:T(8,128)(2,1)} %broadcast_in_dim.96), calls=%async_computation.4 | async-start | bytes 4194304 | tf_op jit(solution)/shard_map/all_to_all | solution.py:14
  85.0 15.8 %copy-start = (bf16[256,2048]{1,0:T(8,128)(2,1)S(1)}, bf16[256,2048]{1,0:T(8,128)(2,1)}, u32[]{:S(2)}) copy-start(bf16[256,2048]{1,0:T(8,128)(2,1)} %param.6) | copy-start | bytes 3145732
  101.6 12.3 %copy-start.4 = (bf16[256]{0:T(256)(128)(2,1)S(1)}, bf16[256]{0:T(256)(128)(2,1)}, u32[]{:S(2)}) copy-start(bf16[256]{0:T(256)(128)(2,1)} %param.9) | copy-start | bytes 1540
  101.8 3.8 %collective-permute-start = (f32[256,512]{0,1:T(8,128)S(1)}, f32[256,512]{0,1:T(8,128)S(1)}, u32[]{:S(2)}, u32[]{:S(2)}) collective-permute-start(f32[256,512]{0,1:T(8,128)S(1)} %pad_maximum_fusion.1), channel_id=1, source_target_pairs={{0,1},{1,0},{2,3},{3,2},{4,5},{5,4},{6,7},{7,6},{8,9},{9,8},{10,11... | collective-permute-start | bytes 1572872 | tf_op jit(solution)/shard_map/ppermute | solution.py:99
  105.7 16.2 %collective-permute-start.1 = (bf16[256,256]{0,1:T(8,128)(2,1)S(1)}, bf16[256,256]{0,1:T(8,128)(2,1)S(1)}, u32[]{:S(2)}, u32[]{:S(2)}) collective-permute-start(bf16[256,256]{0,1:T(8,128)(2,1)S(1)} %select_convert_fusion), channel_id=1, source_target_pairs={{0,2},{2,0},{1,3},{3,1},{4,6},{6,4},{5,7},{7,5},{8,10},{10,8},{9,1... | collective-permute-start | bytes 393224 | tf_op jit(solution)/shard_map/ppermute | solution.py:102
  122.3 40.0 %copy-start.3 = (s32[256]{0:T(256)S(1)}, s32[256]{0:T(256)}, u32[]{:S(2)}) copy-start(s32[256]{0:T(256)} %param.11) | copy-start | bytes 3076
  122.4 6.9 %collective-permute-start.2 = (bf16[256,256]{0,1:T(8,128)(2,1)S(1)}, bf16[256,256]{0,1:T(8,128)(2,1)S(1)}, u32[]{:S(2)}, u32[]{:S(2)}) collective-permute-start(bf16[256,256]{0,1:T(8,128)(2,1)S(1)} %pad_maximum_fusion.2), channel_id=1, source_target_pairs={{0,32},{32,64},{64,96},{96,128},{128,160},{160,192},{192,224},{224... | collective-permute-start | bytes 393224 | tf_op jit(solution)/shard_map/ppermute | solution.py:18
  126.5 90.7 %copy-start.1 = (bf16[256,256]{1,0:T(8,128)(2,1)}, bf16[256,256]{1,0:T(8,128)(2,1)S(1)}, u32[]{:S(2)}) copy-start(bf16[256,256]{1,0:T(8,128)(2,1)S(1)} %copy.13) | copy-start | bytes 393220
  126.5 90.7 %copy-start.2 = (bf16[256,1024]{1,0:T(8,128)(2,1)S(1)}, bf16[256,1024]{1,0:T(8,128)(2,1)}, u32[]{:S(2)}) copy-start(bf16[256,1024]{1,0:T(8,128)(2,1)} %param.7) | copy-start | bytes 1572868
  130.5 87.2 %all-to-all-start.5 = ((bf16[8,256,256]{2,1,0:T(8,128)(2,1)}), bf16[8,256,256]{2,1,0:T(8,128)(2,1)S(1)}, u32[]{:S(2)}, u32[]{:S(2)}) async-start(bf16[8,256,256]{2,1,0:T(8,128)(2,1)} %broadcast_select_fusion), calls=%async_computation.5 | async-start | bytes 2097152 | tf_op jit(solution)/shard_map/all_to_all | solution.py:112
  217.8 24.5 %collective-permute-start.3 = (bf16[9,256,256]{2,1,0:T(8,128)(2,1)S(1)}, bf16[9,256,256]{2,1,0:T(8,128)(2,1)S(1)}, u32[]{:S(2)}, u32[]{:S(2)}) collective-permute-start(bf16[9,256,256]{2,1,0:T(8,128)(2,1)S(1)} %pad_maximum_fusion), channel_id=1, source_target_pairs={{0,32},{32,64},{64,96},{96,128},{128,160},{160,192},{192,224},{224... | collective-permute-start | bytes 3538952 | tf_op jit(solution)/shard_map/ppermute | solution.py:18

commit v2 on v1

v2 whole, which is shorter than its diff:
```python
import functools

import jax
import jax.numpy as jnp
import numpy as np
from jax import lax
from jax.experimental import pallas as pl
from jax.experimental.pallas import tpu as pltpu
from jax.sharding import Mesh, PartitionSpec as P

rope_base = 1000000.0
NY, NX, NP = 4, 4, 4
ROWS = NY * NX
PAIRS = ROWS * NP
SEGS = 16
EXTRA = 128
TOK, HEAD, GROUP = 256, 128, 8
PAIR = 2 * TOK
LOG2E = 1.4426950408889634


def gathered(part, axis, count):
    copies = jnp.broadcast_to(part[None], (count,) + part.shape)
    return lax.all_to_all(copies, axis, 0, 0, tiled=True)


def next_row(value, steps):
    return lax.ppermute(value, ("y", "x"), [(i, i + steps) for i in range(ROWS - steps)])


def pairs_back(value, steps):
    moves = [(i, i + steps) for i in range(PAIRS - steps)]
    return lax.ppermute(value, ("y", "x", "zp"), moves)


def swapped(value, axis):
    return lax.ppermute(value, axis, [(0, 1), (1, 0)])


def column_order(parity):
    matrix = np.zeros((HEAD, HEAD), np.float32)
    for d in range(HEAD):
        x, z, j = d // 64, (d % 64) // 8, d % 8
        other = (z % 2) ^ parity
        matrix[d, other * 64 + x * 32 + (z // 2) * 8 + j] = 1.0
    return matrix


def flash_kernel(mine_sizes, theirs_sizes, first, last, base_ref, q_ref, start_ref, *refs):
    mine = [(ref, n) for ref, size in zip(refs, mine_sizes) for n in range(size)]
    refs = refs[len(mine_sizes) :]
    theirs = [(ref, n) for ref, size in zip(refs, theirs_sizes) for n in range(size)]
    refs = refs[len(theirs_sizes) :]
    order_ref = refs[0]
    refs = refs[1:]
    if not first:
        m_in, l_in, o_in = refs[:3]
        refs = refs[3:]
    count = len(mine)
    lanes = lax.broadcasted_iota(jnp.int32, (TOK, HEAD), 1)
    rows = lax.broadcasted_iota(jnp.int32, (TOK, HEAD), 0)
    factor = HEAD ** (-0.5) * LOG2E
    if first:
        own = pl.ds(pl.multiple_of(base_ref[count + 1], TOK), TOK)
        held = jnp.concatenate([mine[0][0][0, own, :], theirs[0][0][0, own, :]], axis=1)
        cache = jnp.dot(held, order_ref[...], preferred_element_type=jnp.float32)
        refs[3][...] = cache.astype(jnp.bfloat16)

    def keys_of(b):
        (one, n), (two, m) = mine[b], theirs[b]
        return jnp.concatenate([one[n], two[m]], axis=1)

    for h in range(GROUP):
        cols = slice(h * HEAD, (h + 1) * HEAD)
        q = q_ref[:, 2 * h * HEAD : 2 * (h + 1) * HEAD]
        tiles = []
        for b in range(count):
            s = lax.dot_general(
                q, keys_of(b), (((1,), (1,)), ((), ())), preferred_element_type=jnp.float32
            )
            for part in range(PAIR // HEAD):
                t = s[:, part * HEAD : (part + 1) * HEAD]
                key = lanes + (base_ref[b] + part * HEAD)
                ok = key >= start_ref[...]
                if first and b == 0:
                    ok = ok & (key <= rows + base_ref[count])
                tiles.append(jnp.where(ok, t, -jnp.inf))
        top = functools.reduce(jnp.maximum, tiles)
        peak = jnp.max(top, axis=1, keepdims=True)
        if not first:
            old = m_in[h][:, :1]
            peak = jnp.maximum(peak, old)
        peak = jnp.maximum(peak, -1e30)
        wide = jnp.broadcast_to(peak, (TOK, HEAD))
        probs = [jnp.exp2((t - wide) * factor) for t in tiles]
        total = jnp.sum(functools.reduce(jnp.add, probs), axis=1, keepdims=True)
        mixed = None
        per = PAIR // HEAD
        for b in range(count):
            p = jnp.concatenate(probs[per * b : per * (b + 1)], axis=1).astype(jnp.bfloat16)
            d = jnp.dot(p, keys_of(b), preferred_element_type=jnp.float32)
            mixed = d if mixed is None else mixed + d
        half = HEAD // 2
        mixed = jnp.concatenate([mixed[:, half:HEAD], mixed[:, HEAD + half :]], axis=1)
        if not first:
            scale = jnp.exp2((old - peak) * factor)
            total = total + l_in[h][:, :1] * scale
            mixed = mixed + o_in[:, cols] * scale
        if last:
            refs[1][h * TOK : (h + 1) * TOK, :] = (mixed * (1.0 / total)).astype(jnp.bfloat16)
        else:
            refs[0][h] = jnp.broadcast_to(peak, (TOK, HEAD))
            refs[1][h] = jnp.broadcast_to(total, (TOK, HEAD))
            refs[2][:, cols] = mixed
    if last:
        for h in range(GROUP):
            rows_of = slice(h * TOK, (h + 1) * TOK)
            placed = jnp.dot(refs[1][rows_of, :], order_ref[...], preferred_element_type=jnp.float32)
            refs[0][:, h * HEAD : (h + 1) * HEAD] = placed.astype(jnp.bfloat16)


def flash(queries, start, scalars, mine, theirs, order, state):
    first = state is None
    vmem = pl.BlockSpec(memory_space=pltpu.VMEM)
    operands = [queries, start, *mine, *theirs, order, *(state or ())]
    if first:
        out = [jax.ShapeDtypeStruct((GROUP, TOK, HEAD), jnp.float32)] * 2
        out.append(jax.ShapeDtypeStruct((TOK, GROUP * HEAD), jnp.float32))
        out.append(jax.ShapeDtypeStruct((TOK, 2 * HEAD), jnp.bfloat16))
    else:
        out = [jax.ShapeDtypeStruct((TOK, GROUP * HEAD), jnp.bfloat16)]
    mine_sizes = [m.shape[0] for m in mine]
    theirs_sizes = [m.shape[0] for m in theirs]
    keys = sum(mine_sizes) * PAIR
    return pl.pallas_call(
        functools.partial(flash_kernel, mine_sizes, theirs_sizes, first, not first),
        out_shape=out,
        in_specs=[pl.BlockSpec(memory_space=pltpu.SMEM)] + [vmem] * len(operands),
        out_specs=[vmem] * len(out),
        scratch_shapes=[] if first else [pltpu.VMEM((GROUP * TOK, HEAD), jnp.bfloat16)],
        compiler_params=pltpu.CompilerParams(vmem_limit_bytes=40 * 1024 * 1024),
        cost_estimate=pl.CostEstimate(
            flops=8 * GROUP * TOK * keys * HEAD,
            bytes_accessed=4 << 20,
            transcendentals=GROUP * TOK * keys,
        ),
    )(jnp.stack(scalars), *operands)


def body(hidden, queries, kv_weight, kv_bias, window, segment_ids):
    feats = hidden.shape[1]
    pz = lax.axis_index("zp")
    parity = lax.axis_index("zq")
    row = lax.axis_index("y") * NX + lax.axis_index("x")
    zh = lax.axis_index("zh")
    core = lax.axis_index("core")
    even = parity == 0
    pair = row * NP + pz
    pair_pos = pair * PAIR + jnp.arange(PAIR, dtype=jnp.int32)
    base = pair * PAIR + parity * TOK
    positions = base + jnp.arange(TOK, dtype=jnp.int32)

    partner = swapped(hidden, "zq")
    tokens = jnp.concatenate(
        [jnp.where(even, hidden, partner), jnp.where(even, partner, hidden)], axis=0
    )

    ids = jnp.arange(SEGS, dtype=jnp.int32)
    below = jnp.sum((segment_ids[:, None] < ids[None, :]).astype(jnp.float32), axis=0)
    below = jnp.pad(below.astype(jnp.bfloat16), (0, EXTRA - SEGS))

    count = kv_weight.shape[1]
    beside = jnp.broadcast_to(below[None, :], (count, EXTRA))
    line = gathered(jnp.concatenate([kv_weight.T, beside], axis=1), "zp", NP)
    whole = gathered(line, ("y", "x"), ROWS).reshape(-1, feats + EXTRA)
    terms = lax.dot_general(
        tokens, whole[:, :feats], (((1,), (1,)), ((), ())), preferred_element_type=jnp.float32
    )
    counted = jnp.sum(whole[::count, feats : feats + SEGS].astype(jnp.float32), axis=0)
    high = jnp.floor(counted / 128.0)
    digits = jnp.concatenate([high, counted - 128.0 * high]).astype(jnp.bfloat16)

    quarter = [terms[:, g * HEAD : (g + 1) * HEAD] for g in range(4)]
    lower = core == 0
    sent = jnp.concatenate(
        [jnp.where(lower, quarter[1], quarter[0]), jnp.where(lower, quarter[3], quarter[2])], axis=1
    )
    kept = jnp.concatenate(
        [jnp.where(lower, quarter[0], quarter[1]), jnp.where(lower, quarter[2], quarter[3])], axis=1
    )
    chip = kept + swapped(sent, "core")
    near = zh == 0
    far = jnp.where(near, chip[:, HEAD:], chip[:, :HEAD]).astype(jnp.bfloat16)
    far = swapped(far, "zh")
    projected = jnp.where(near, chip[:, :HEAD], chip[:, HEAD:]) + far.astype(jnp.float32)

    def of_parity(values):
        parts = values.reshape(-1, NP, 2, 8)
        return jnp.where(even, parts[:, :, 0], parts[:, :, 1]).reshape(-1)

    projected = projected + of_parity(kv_bias.astype(jnp.float32))[None, :]
    freqs = rope_base ** (-2.0 * jnp.arange(HEAD // 2, dtype=jnp.float32) / HEAD)
    angles = pair_pos.astype(jnp.float32)[:, None] * of_parity(freqs)[None, :]
    cosine = jnp.cos(angles)
    sine = jnp.sin(angles)
    former = projected[:, :32]
    latter = projected[:, 32:64]
    unit = jnp.concatenate(
        [former * cosine - latter * sine, latter * cosine + former * sine, projected[:, 64:]], axis=1
    ).astype(jnp.bfloat16)

    back = [pairs_back(unit, steps) for steps in (1, 2, 3)]
    back8 = next_row(unit, 2)
    near_mine = jnp.stack([unit] + back)
    tail = jnp.zeros((16, HEAD), jnp.bfloat16).at[0, : 2 * SEGS].set(digits)
    packed = jnp.concatenate([unit] + back + [back8, tail], axis=0)
    packed_theirs = swapped(packed, "zq")
    near_theirs = packed_theirs[: 5 * PAIR].reshape(5, PAIR, HEAD)
    far_mine = next_row(near_mine, 1)
    far_theirs = [next_row(near_theirs[:2], 1), swapped(far_mine[2:], "zq")]

    digits = packed_theirs[5 * PAIR, : 2 * SEGS].astype(jnp.float32)
    doc_start = (counted + 128.0 * digits[:SEGS] + digits[SEGS:]).astype(jnp.int32)
    token_start = jnp.sum(
        jnp.where(segment_ids[:, None] == ids[None, :], doc_start[None, :], 0), axis=1
    )
    token_start = jnp.maximum(token_start, positions - window[0] + 1)

    order = jnp.where(
        even,
        jnp.asarray(column_order(0), jnp.bfloat16),
        jnp.asarray(column_order(1), jnp.bfloat16),
    )
    gap = jnp.zeros((HEAD, HEAD // 2), jnp.bfloat16)
    spread = jnp.concatenate([order[:, : HEAD // 2], gap, order[:, HEAD // 2 :], gap], axis=1)
    wide_q = jnp.dot(
        queries.reshape(TOK * GROUP, HEAD), spread, preferred_element_type=jnp.float32
    ).astype(jnp.bfloat16)
    wide_q = wide_q.reshape(TOK, 2 * GROUP * HEAD)
    back_order = order.T

    half = HEAD // 2
    none = jnp.zeros((half, HEAD), jnp.bfloat16)
    cache_order = jnp.concatenate(
        [
            jnp.concatenate([back_order[:half], none, back_order[half:], none], axis=0),
            jnp.concatenate([none, back_order[:half], none, back_order[half:]], axis=0),
        ],
        axis=1,
    )
    start = jnp.broadcast_to(token_start[:, None], (TOK, HEAD))
    scalars = [(pair - steps) * PAIR for steps in (0, 1, 2, 3, 8)] + [base, parity * TOK]
    near_all = packed[: 5 * PAIR].reshape(5, PAIR, HEAD)
    *state, cache = flash(wide_q, start, scalars, [near_all], [near_theirs], cache_order, None)
    scalars = [(pair - steps) * PAIR for steps in (4, 5, 6, 7)]
    (attended,) = flash(wide_q, start, scalars, [far_mine], far_theirs, back_order, state)
    return (attended, cache)


def solution(mesh):
    axes = ("y", "x", "zp", "zq", "zh", "core")
    fine = Mesh(mesh.devices.reshape(NY, NX, NP, 2, 2, 2), axes)
    ctx, tp = ("y", "x", "zp", "zq"), ("zh", "core")
    in_specs = (P(ctx, tp), P(ctx, tp), P(tp, ctx), P(tp), P(tp), P(ctx))
    out_specs = (P(ctx, tp), P(ctx, tp))
    return jax.shard_map(body, mesh=fine, in_specs=in_specs, out_specs=out_specs, check_vma=False)
```

time: 268 us -> 182 us (0.68)
  blocking collectives: 128 us -> 23.7 us
  starting transfers between devices: 43.3 us -> 70.8 us
  matrix products: 24.6 us -> 3.25 us
  Pallas kernels: 0 us -> 19.5 us
  between operations: 12 us -> 1.7 us
  other arithmetic: 7.82 us -> 10.8 us
    psum x1 -> x0, blocking collectives: 54.1 us -> none  [body(): doc_start = lax.psum(below, ('y', 'x', 'zl'))]
    all_to_all x4 -> x1, blocking collectives: 73.4 us -> 23.7 us  [gathered(): return lax.all_to_all(copies, axis, 0, 0, tiled=True)]
    ppermute x4 -> x11, starting transfers between devices: 16.2 us -> 63.3 us  [the longest x3 23.6 us: pairs_back(): return lax.ppermute(value, ('y', 'x', 'zp'), moves)]
    dot_general x36 -> x2, matrix products: 24.6 us -> 3.25 us  [the longest x1 2.82 us: body(): lax.dot_general(tokens, whole[:, :feats], (((1,), (1,)), ((), ())), prefe...]
    all_to_all x1 -> x0, starting transfers between devices: 20.6 us -> none  [body(): recent = lax.all_to_all(outgoing, 'zl', 0, 0, tiled=True)]
    pallas_call x0 -> x2, Pallas kernels: none -> 19.5 us  [flash(): pl.pallas_call(functools.partial(flash_kernel, mine_sizes, theirs_sizes,...]
    all_to_all x1, waiting for transfers between devices: 14 us -> 0.01 us  [gathered(): return lax.all_to_all(copies, axis, 0, 0, tiled=True)]
    ppermute x4 -> x11, waiting for transfers between devices: 29.9 us -> 41.8 us  [the longest x5 26.7 us: swapped(): return lax.ppermute(value, axis, [(0, 1), (1, 0)])]
  transfers between devices with their start and end apart: 6 -> 12, of which waited for: 5 -> 5; matrix products, arithmetic and copies ran while one was open for 3% -> 7% of each run, Pallas kernels for 0% -> 6%
where the time goes in v2:
time: 182 us; the launch traced here: 181 us
  starting transfers between devices  70.8 us (39%)
  waiting for transfers between devices  41.8 us (23%)
  blocking collectives  23.7 us (13%)
  Pallas kernels  19.5 us (11%)
  other arithmetic  10.8 us (6%)
  local copies, waits for them, and re-layouts  9.11 us (5%)
  matrix products  3.25 us (2%)
    ppermute x5, waiting for transfers between devices, swapped(): return lax.ppermute(value, axis, [(0, 1), (1, 0)])  26.7 us
    all_to_all x1, blocking collectives, gathered(): return lax.all_to_all(copies, axis, 0, 0, tiled=True)  23.7 us
    ppermute x3, starting transfers between devices, pairs_back(): return lax.ppermute(value, ('y', 'x', 'zp'), moves)  23.6 us
    ppermute x5, starting transfers between devices, swapped(): return lax.ppermute(value, axis, [(0, 1), (1, 0)])  22.7 us
    pallas_call x2, Pallas kernels, flash(): pl.pallas_call(functools.partial(flash_kernel, mine_sizes, theirs_sizes,...  19.5 us
    ppermute x3, starting transfers between devices, next_row(): lax.ppermute(value, ('y', 'x'), [(i, i + steps) for i in range(ROWS - ste...  16.9 us
    ppermute x3, waiting for transfers between devices, next_row(): lax.ppermute(value, ('y', 'x'), [(i, i + steps) for i in range(ROWS - ste...  8.98 us
    all_to_all x1, starting transfers between devices, gathered(): return lax.all_to_all(copies, axis, 0, 0, tiled=True)  7.55 us
  transfers between devices with their start and end apart: 12, of which 5 were waited for; matrix products, arithmetic and copies ran while one was open for 7% of the time, Pallas kernels for 6%

profile of v2, /device:TPU:6, one launch (start us, length us, event | category | flops | bytes accessed | tf_op | source)
XLA Modules:
  0.0 180.8 jit_solution(12891262688554394800)
XLA Ops:
  2.2 23.7 %all_to_all.10 = bf16[4,8,2176]{2,1,0:T(8,128)(2,1)S(1)} all-to-all(bf16[4,8,2176]{2,1,0:T(8,128)(2,1)S(1)} %broadcast_in_dim.22), channel_id=1, replica_groups=mesh['y'=4,'x'=4,'zp'=4,'zq'=2,'zh'=2,'core'=2] {'zp'}, dimensions={0} | all-to-all | bytes 278528 | tf_op jit(solution)/shard_map/all_to_all | solution.py:24
  25.9 1.5 broadcast_in_dim.23
  27.5 7.6 %all-to-all-start.1 = ((bf16[16,4,8,2176]{3,2,1,0:T(8,128)(2,1)}), bf16[16,4,8,2176]{3,2,1,0:T(8,128)(2,1)S(1)}, u32[]{:S(2)}, u32[]{:S(2)}) async-start(bf16[16,4,8,2176]{3,2,1,0:T(8,128)(2,1)} %broadcast_in_dim.23), calls=%async_computation.1 | async-start | bytes 4456448 | tf_op jit(solution)/shard_map/all_to_all | solution.py:24
  35.0 2.6 %collective-permute-start = (bf16[256,2048]{1,0:T(8,128)(2,1)}, bf16[256,2048]{1,0:T(8,128)(2,1)}, u32[]{:S(2)}, u32[]{:S(2)}) collective-permute-start(bf16[256,2048]{1,0:T(8,128)(2,1)} %param.10), channel_id=1, source_target_pairs={{0,4},{4,0},{1,5},{5,1},{2,6},{6,2},{3,7},{7,3},{8,12},{12,8},{9,1... | collective-permute-start | bytes 3145736 | tf_op jit(solution)/shard_map/ppermute | solution.py:37
  38.2 20.0 %collective-permute-done = bf16[256,2048]{1,0:T(8,128)(2,1)} collective-permute-done((bf16[256,2048]{1,0:T(8,128)(2,1)}, bf16[256,2048]{1,0:T(8,128)(2,1)}, u32[]{:S(2)}, u32[]{:S(2)}) %collective-permute-start) | collective-permute-done | bytes 1048608 | tf_op jit(solution)/shard_map/ppermute | solution.py:37
  58.2 3.1 %broadcast_select_fusion.1 = (bf16[256,2048]{1,0:T(8,128)(2,1)}, bf16[256,2048]{1,0:T(8,128)(2,1)}) fusion(bf16[256,2048]{1,0:T(8,128)(2,1)} %param.10, bf16[256,2048]{1,0:T(8,128)(2,1)} %collective-permute-done, pred[]{:T(512)S(6)} %eq.24), kind=kLoop, calls=%fused_computation.8 | loop fusion | flops 1048576 | bytes 4194305 | tf_op jit(solution)/shard_map/jit(_where)/select_n | solution.py:165
  61.3 2.8 %fusion.1 = f32[512,512]{1,0:T(8,128)S(1)} fusion(bf16[512,2176]{1,0:T(8,128)(2,1)S(1)} %bitcast.46, bf16[256,2048]{1,0:T(8,128)(2,1)} %get-tuple-element.25, bf16[256,2048]{1,0:T(8,128)(2,1)} %get-tuple-element.24), kind=kOutput, calls=%fused_computation.2 | convolution fusion | flops 1077936128 | bytes 5242880 | tf_op jit(solution)/shard_map/dot_general | solution.py:176
  65.0 1.9 %collective-permute-start.1 = (f32[512,256]{1,0:T(8,128)}, f32[512,256]{1,0:T(8,128)}, u32[]{:S(2)}, u32[]{:S(2)}) collective-permute-start(f32[512,256]{1,0:T(8,128)} %pad_maximum_fusion), channel_id=1, source_target_pairs={{0,1},{1,0},{2,3},{3,2},{4,5},{5,4},{6,7},{7,6},{8,9},{9,8},{10,11... | collective-permute-start | bytes 1572872 | tf_op jit(solution)/shard_map/ppermute | solution.py:37
  67.3 1.9 %collective-permute-done.1 = f32[512,256]{1,0:T(8,128)} collective-permute-done((f32[512,256]{1,0:T(8,128)}, f32[512,256]{1,0:T(8,128)}, u32[]{:S(2)}, u32[]{:S(2)}) %collective-permute-start.1) | collective-permute-done | bytes 524320 | tf_op jit(solution)/shard_map/ppermute | solution.py:37
  70.3 11.6 %collective-permute-start.2 = (bf16[512,128]{1,0:T(8,128)(2,1)S(1)}, bf16[512,128]{1,0:T(8,128)(2,1)S(1)}, u32[]{:S(2)}, u32[]{:S(2)}) collective-permute-start(bf16[512,128]{1,0:T(8,128)(2,1)S(1)} %select_convert_fusion), channel_id=1, source_target_pairs={{0,2},{2,0},{1,3},{3,1},{4,6},{6,4},{5,7},{7,5},{8,10},{10,8},{9,1... | collective-permute-start | bytes 393224 | tf_op jit(solution)/shard_map/ppermute | solution.py:37
  81.9 4.8 %collective-permute-done.2 = bf16[512,128]{1,0:T(8,128)(2,1)S(1)} collective-permute-done((bf16[512,128]{1,0:T(8,128)(2,1)S(1)}, bf16[512,128]{1,0:T(8,128)(2,1)S(1)}, u32[]{:S(2)}, u32[]{:S(2)}) %collective-permute-start.2) | collective-permute-done | bytes 131104 | tf_op jit(solution)/shard_map/ppermute | solution.py:37
  86.9 1.2 fusion.11
  88.3 5.3 %collective-permute-start.3 = (bf16[512,128]{1,0:T(8,128)(2,1)S(1)}, bf16[512,128]{1,0:T(8,128)(2,1)S(1)}, u32[]{:S(2)}, u32[]{:S(2)}) collective-permute-start(bf16[512,128]{1,0:T(8,128)(2,1)S(1)} %get-tuple-element.23), channel_id=1, source_target_pairs={{0,8},{8,16},{16,24},{24,32},{32,40},{40,48},{48,56},{56,64},{64,7... | collective-permute-start | bytes 393224 | tf_op jit(solution)/shard_map/ppermute | solution.py:33
  93.6 12.1 %collective-permute-start.4 = (bf16[512,128]{1,0:T(8,128)(2,1)S(1)}, bf16[512,128]{1,0:T(8,128)(2,1)S(1)}, u32[]{:S(2)}, u32[]{:S(2)}) collective-permute-start(bf16[512,128]{1,0:T(8,128)(2,1)S(1)} %get-tuple-element.23), channel_id=1, source_target_pairs={{0,16},{8,24},{16,32},{24,40},{32,48},{40,56},{48,64},{56,72},{64,... | collective-permute-start | bytes 393224 | tf_op jit(solution)/shard_map/ppermute | solution.py:33
  105.7 6.3 %collective-permute-start.5 = (bf16[512,128]{1,0:T(8,128)(2,1)S(1)}, bf16[512,128]{1,0:T(8,128)(2,1)S(1)}, u32[]{:S(2)}, u32[]{:S(2)}) collective-permute-start(bf16[512,128]{1,0:T(8,128)(2,1)S(1)} %get-tuple-element.23), channel_id=1, source_target_pairs={{0,24},{8,32},{16,40},{24,48},{32,56},{40,64},{48,72},{56,80},{64,... | collective-permute-start | bytes 393224 | tf_op jit(solution)/shard_map/ppermute | solution.py:33
  112.0 2.3 %collective-permute-start.6 = (bf16[512,128]{1,0:T(8,128)(2,1)S(1)}, bf16[512,128]{1,0:T(8,128)(2,1)S(1)}, u32[]{:S(2)}, u32[]{:S(2)}) collective-permute-start(bf16[512,128]{1,0:T(8,128)(2,1)S(1)} %get-tuple-element.23), channel_id=1, source_target_pairs={{0,64},{32,96},{64,128},{96,160},{128,192},{160,224},{192,256},{22... | collective-permute-start | bytes 393224 | tf_op jit(solution)/shard_map/ppermute | solution.py:28
  115.7 6.1 %collective-permute-done.4 = bf16[512,128]{1,0:T(8,128)(2,1)S(1)} collective-permute-done((bf16[512,128]{1,0:T(8,128)(2,1)S(1)}, bf16[512,128]{1,0:T(8,128)(2,1)S(1)}, u32[]{:S(2)}, u32[]{:S(2)}) %collective-permute-start.4) | collective-permute-done | bytes 131104 | tf_op jit(solution)/shard_map/ppermute | solution.py:33
  124.5 4.5 %collective-permute-start.7 = (bf16[2576,128]{1,0:T(8,128)(2,1)}, bf16[2576,128]{1,0:T(8,128)(2,1)}, u32[]{:S(2)}, u32[]{:S(2)}) collective-permute-start(bf16[2576,128]{1,0:T(8,128)(2,1)} %constant_dynamic-update-slice_fusion), channel_id=1, source_target_pairs={{0,4},{4,0},{1,5},{5,1},{2,6},{6,2},{3,7},{7,3},{8,12},{12,8},{9,1... | collective-permute-start | bytes 1978376 | tf_op jit(solution)/shard_map/ppermute | solution.py:37
  129.9 8.1 %collective-permute-start.8 = (bf16[4,512,128]{2,1,0:T(8,128)(2,1)}, bf16[4,512,128]{2,1,0:T(8,128)(2,1)S(1)}, u32[]{:S(2)}, u32[]{:S(2)}) collective-permute-start(bf16[4,512,128]{2,1,0:T(8,128)(2,1)} %pad_maximum_fusion.1), channel_id=1, source_target_pairs={{0,32},{32,64},{64,96},{96,128},{128,160},{160,192},{192,224},{224... | collective-permute-start | bytes 1572872 | tf_op jit(solution)/shard_map/ppermute | solution.py:28
  140.4 9.0 %collective-permute-done.8.refs_0_ = bf16[4,512,128]{2,1,0:T(8,128)(2,1)S(1)} collective-permute-done((bf16[4,512,128]{2,1,0:T(8,128)(2,1)}, bf16[4,512,128]{2,1,0:T(8,128)(2,1)S(1)}, u32[]{:S(2)}, u32[]{:S(2)}) %collective-permute-start.8) | collective-permute-done | bytes 524320 | tf_op jit(solution)/shard_map/ppermute | solution.py:28
  149.4 2.2 %collective-permute-start.10 = (bf16[2,512,128]{2,1,0:T(8,128)(2,1)S(1)}, bf16[2,512,128]{2,1,0:T(8,128)(2,1)S(1)}, u32[]{:S(2)}, u32[]{:S(2)}) collective-permute-start(bf16[2,512,128]{2,1,0:T(8,128)(2,1)S(1)} %slice.150), channel_id=1, source_target_pairs={{0,4},{4,0},{1,5},{5,1},{2,6},{6,2},{3,7},{7,3},{8,12},{12,8},{9,1... | collective-permute-start | bytes 786440 | tf_op jit(solution)/shard_map/ppermute | solution.py:37
  153.4 6.6 %collective-permute-start.9 = (bf16[2,512,128]{2,1,0:T(8,128)(2,1)S(1)}, bf16[2,512,128]{2,1,0:T(8,128)(2,1)S(1)}, u32[]{:S(2)}, u32[]{:S(2)}) collective-permute-start(bf16[2,512,128]{2,1,0:T(8,128)(2,1)S(1)} %bitcast.53), channel_id=1, source_target_pairs={{0,32},{32,64},{64,96},{96,128},{128,160},{160,192},{192,224},{224... | collective-permute-start | bytes 786440 | tf_op jit(solution)/shard_map/ppermute | solution.py:28
  161.2 10.0 %shard_map.95 = (f32[8,256,128]{2,1,0:T(8,128)S(1)}, f32[8,256,128]{2,1,0:T(8,128)S(1)}, f32[256,1024]{1,0:T(8,128)S(1)}, bf16[256,256]{1,0:T(8,128)(2,1)}) custom-call(s32[7]{0:T(128)S(1)} %stack.68.base_ref, bf16[256,2048]{1,0:T(8,128)(2,1)S(1)} %reshape.198.q_ref, s32[256,128]{1,0:T(8,128)S(1)} %broadcast_in_dim.30.start_ref, ...), custom_call_target="tpu_custom_call" | custom-call | flops 5368709120 | bytes 4194304 | tf_op jit(solution)/shard_map/pallas_call | solution.py:135
  171.3 9.5 %shard_map.96 = bf16[256,1024]{1,0:T(8,128)(2,1)} custom-call(s32[4]{0:T(128)S(1)} %pad_add_fusion.base_ref, bf16[256,2048]{1,0:T(8,128)(2,1)S(1)} %reshape.198.q_ref, s32[256,128]{1,0:T(8,128)S(1)} %broadcast_in_dim.30.start_ref, bf16[4,512,128]{2,1,0:T(8,128)(2,1)S(1)} %collective-permute-done.8.refs_0_, ...), custom_call_target="tpu_custom_call" | custom-call | flops 4294967296 | bytes 4194304 | tf_op jit(solution)/shard_map/pallas_call | solution.py:135
  (67 shorter events, 14.6 us)
Async XLA Ops:
  27.5 10.1 %copy-start = (bf16[256,1024]{1,0:T(8,128)(2,1)S(1)}, bf16[256,1024]{1,0:T(8,128)(2,1)}, u32[]{:S(2)}) copy-start(bf16[256,1024]{1,0:T(8,128)(2,1)} %param.11) | copy-start | bytes 1572868
  27.5 10.4 %copy-start.4 = (bf16[256]{0:T(256)(128)(2,1)S(1)}, bf16[256]{0:T(256)(128)(2,1)}, u32[]{:S(2)}) copy-start(bf16[256]{0:T(256)(128)(2,1)} %param.13) | copy-start | bytes 1540
  27.5 33.8 %all-to-all-start.1 = ((bf16[16,4,8,2176]{3,2,1,0:T(8,128)(2,1)}), bf16[16,4,8,2176]{3,2,1,0:T(8,128)(2,1)S(1)}, u32[]{:S(2)}, u32[]{:S(2)}) async-start(bf16[16,4,8,2176]{3,2,1,0:T(8,128)(2,1)} %broadcast_in_dim.23), calls=%async_computation.1 | async-start | bytes 4456448 | tf_op jit(solution)/shard_map/all_to_all | solution.py:24
  35.0 23.2 %collective-permute-start = (bf16[256,2048]{1,0:T(8,128)(2,1)}, bf16[256,2048]{1,0:T(8,128)(2,1)}, u32[]{:S(2)}, u32[]{:S(2)}) collective-permute-start(bf16[256,2048]{1,0:T(8,128)(2,1)} %param.10), channel_id=1, source_target_pairs={{0,4},{4,0},{1,5},{5,1},{2,6},{6,2},{3,7},{7,3},{8,12},{12,8},{9,1... | collective-permute-start | bytes 3145736 | tf_op jit(solution)/shard_map/ppermute | solution.py:37
  64.1 2.9 %copy-start.1 = (bf16[128,128]{0,1:T(8,128)(2,1)S(1)}, bf16[128,128]{0,1:T(8,128)(2,1)}, u32[]{:S(2)}) copy-start(bf16[128,128]{0,1:T(8,128)(2,1)} %constant.106.clone) | copy-start | bytes 98308
  64.1 2.9 %copy-start.2 = (bf16[128,128]{0,1:T(8,128)(2,1)S(1)}, bf16[128,128]{0,1:T(8,128)(2,1)}, u32[]{:S(2)}) copy-start(bf16[128,128]{0,1:T(8,128)(2,1)} %constant.107.clone) | copy-start | bytes 98308
  65.0 4.1 %collective-permute-start.1 = (f32[512,256]{1,0:T(8,128)}, f32[512,256]{1,0:T(8,128)}, u32[]{:S(2)}, u32[]{:S(2)}) collective-permute-start(f32[512,256]{1,0:T(8,128)} %pad_maximum_fusion), channel_id=1, source_target_pairs={{0,1},{1,0},{2,3},{3,2},{4,5},{5,4},{6,7},{7,6},{8,9},{9,8},{10,11... | collective-permute-start | bytes 1572872 | tf_op jit(solution)/shard_map/ppermute | solution.py:37
  70.3 16.5 %collective-permute-start.2 = (bf16[512,128]{1,0:T(8,128)(2,1)S(1)}, bf16[512,128]{1,0:T(8,128)(2,1)S(1)}, u32[]{:S(2)}, u32[]{:S(2)}) collective-permute-start(bf16[512,128]{1,0:T(8,128)(2,1)S(1)} %select_convert_fusion), channel_id=1, source_target_pairs={{0,2},{2,0},{1,3},{3,1},{4,6},{6,4},{5,7},{7,5},{8,10},{10,8},{9,1... | collective-permute-start | bytes 393224 | tf_op jit(solution)/shard_map/ppermute | solution.py:37
  88.3 26.7 %collective-permute-start.3 = (bf16[512,128]{1,0:T(8,128)(2,1)S(1)}, bf16[512,128]{1,0:T(8,128)(2,1)S(1)}, u32[]{:S(2)}, u32[]{:S(2)}) collective-permute-start(bf16[512,128]{1,0:T(8,128)(2,1)S(1)} %get-tuple-element.23), channel_id=1, source_target_pairs={{0,8},{8,16},{16,24},{24,32},{32,40},{40,48},{48,56},{56,64},{64,7... | collective-permute-start | bytes 393224 | tf_op jit(solution)/shard_map/ppermute | solution.py:33
  93.6 28.3 %collective-permute-start.4 = (bf16[512,128]{1,0:T(8,128)(2,1)S(1)}, bf16[512,128]{1,0:T(8,128)(2,1)S(1)}, u32[]{:S(2)}, u32[]{:S(2)}) collective-permute-start(bf16[512,128]{1,0:T(8,128)(2,1)S(1)} %get-tuple-element.23), channel_id=1, source_target_pairs={{0,16},{8,24},{16,32},{24,40},{32,48},{40,56},{48,64},{56,72},{64,... | collective-permute-start | bytes 393224 | tf_op jit(solution)/shard_map/ppermute | solution.py:33
  105.7 16.8 %collective-permute-start.5 = (bf16[512,128]{1,0:T(8,128)(2,1)S(1)}, bf16[512,128]{1,0:T(8,128)(2,1)S(1)}, u32[]{:S(2)}, u32[]{:S(2)}) collective-permute-start(bf16[512,128]{1,0:T(8,128)(2,1)S(1)} %get-tuple-element.23), channel_id=1, source_target_pairs={{0,24},{8,32},{16,40},{24,48},{32,56},{40,64},{48,72},{56,80},{64,... | collective-permute-start | bytes 393224 | tf_op jit(solution)/shard_map/ppermute | solution.py:33
  112.0 11.2 %collective-permute-start.6 = (bf16[512,128]{1,0:T(8,128)(2,1)S(1)}, bf16[512,128]{1,0:T(8,128)(2,1)S(1)}, u32[]{:S(2)}, u32[]{:S(2)}) collective-permute-start(bf16[512,128]{1,0:T(8,128)(2,1)S(1)} %get-tuple-element.23), channel_id=1, source_target_pairs={{0,64},{32,96},{64,128},{96,160},{128,192},{160,224},{192,256},{22... | collective-permute-start | bytes 393224 | tf_op jit(solution)/shard_map/ppermute | solution.py:28
  124.5 27.1 %collective-permute-start.7 = (bf16[2576,128]{1,0:T(8,128)(2,1)}, bf16[2576,128]{1,0:T(8,128)(2,1)}, u32[]{:S(2)}, u32[]{:S(2)}) collective-permute-start(bf16[2576,128]{1,0:T(8,128)(2,1)} %constant_dynamic-update-slice_fusion), channel_id=1, source_target_pairs={{0,4},{4,0},{1,5},{5,1},{2,6},{6,2},{3,7},{7,3},{8,12},{12,8},{9,1... | collective-permute-start | bytes 1978376 | tf_op jit(solution)/shard_map/ppermute | solution.py:37
  129.9 19.5 %collective-permute-start.8 = (bf16[4,512,128]{2,1,0:T(8,128)(2,1)}, bf16[4,512,128]{2,1,0:T(8,128)(2,1)S(1)}, u32[]{:S(2)}, u32[]{:S(2)}) collective-permute-start(bf16[4,512,128]{2,1,0:T(8,128)(2,1)} %pad_maximum_fusion.1), channel_id=1, source_target_pairs={{0,32},{32,64},{64,96},{96,128},{128,160},{160,192},{192,224},{224... | collective-permute-start | bytes 1572872 | tf_op jit(solution)/shard_map/ppermute | solution.py:28
  138.5 13.9 %copy-start.3 = (s32[256]{0:T(256)S(1)}, s32[256]{0:T(256)}, u32[]{:S(2)}) copy-start(s32[256]{0:T(256)} %param.15) | copy-start | bytes 3076
  149.4 21.8 %collective-permute-start.10 = (bf16[2,512,128]{2,1,0:T(8,128)(2,1)S(1)}, bf16[2,512,128]{2,1,0:T(8,128)(2,1)S(1)}, u32[]{:S(2)}, u32[]{:S(2)}) collective-permute-start(bf16[2,512,128]{2,1,0:T(8,128)(2,1)S(1)} %slice.150), channel_id=1, source_target_pairs={{0,4},{4,0},{1,5},{5,1},{2,6},{6,2},{3,7},{7,3},{8,12},{12,8},{9,1... | collective-permute-start | bytes 786440 | tf_op jit(solution)/shard_map/ppermute | solution.py:37
  153.4 17.8 %collective-permute-start.9 = (bf16[2,512,128]{2,1,0:T(8,128)(2,1)S(1)}, bf16[2,512,128]{2,1,0:T(8,128)(2,1)S(1)}, u32[]{:S(2)}, u32[]{:S(2)}) collective-permute-start(bf16[2,512,128]{2,1,0:T(8,128)(2,1)S(1)} %bitcast.53), channel_id=1, source_target_pairs={{0,32},{32,64},{64,96},{96,128},{128,160},{160,192},{192,224},{224... | collective-permute-start | bytes 786440 | tf_op jit(solution)/shard_map/ppermute | solution.py:28
